TPU v7x, 1024 devices: a whole 8x8x8 slice. The times are simulated.
1024 devices in a mesh: dom: 8 (over y), map: 8 (over z), slab: 16 (over x, core).
Axes of the slice: x: 8, y: 8, z: 8, core: 2. Of those that a mesh axis runs over, the one named last changes fastest.
Arguments:
- particles: bfloat16 [256, 64, 4096], P(('dom', 'map'), 'slab'), may hold values from -6 to 6
- class_list: int32 [256, 2], P(('dom', 'map')), may hold values from 0 to 7, all different within a row; in each aligned block of 4 rows (0 to 3, 4 to 7, ...) at most 2 rows name the same one
- orient: int32 [256, 2], P(('dom', 'map')), may hold values from 0 to 3
- ctf_index: int32 [256], P(('dom', 'map')), may hold values from 0 to 63
- tomo_id: int32 [256], P(('dom', 'map')), may hold values from 0 to 31, as said below
- defocus: float32 [64], replicated, may hold values from 20 to 200
- tomo_gain: float32 [32], replicated, may hold values from 0.5 to 2
- maps: float32 [8, 128, 128, 128], P('map', 'slab'), may hold values from -6 to 6
Outputs:
- real_grad: float32 [8, 128, 128, 128], P('map', None, 'slab')
- scores: float32 [256, 2], P(('dom', 'map'))
Inputs may be any that keep to these rules, and one draw needn't show every extreme that they name: `class_list`: each particle lists 2 different classes; the particles of one device name no class more than 2 times. `tomo_id`: the particles on dom index d belong to tomograms d * 4 to (d + 1) * 4 - 1.
All inputs are finite; a program needn't handle non-finite values.
Results may differ from a plain program's by a relative error of at most 0.0003.
Values may be sent and summed in bfloat16 or wider, within the bound.
A program may use at most 64 MiB of HBM per device.

v0:
```python
import math

import jax
import jax.numpy as jnp
from jax import lax
from jax.sharding import PartitionSpec as P

L = 128
BOX = 64
K = 2


TAU_REG = 0.1
PHASE_SHIFT = 0.1


def wrap_freq(index, grid_size):
    return jnp.where(index < grid_size // 2, index, index - grid_size)


def cas_table(freqs, grid_size):
    points = jnp.arange(grid_size, dtype=jnp.int32)
    phase = freqs[:, None] * points[None, :] % grid_size
    angle = phase.astype(jnp.float32) * (2.0 * math.pi / grid_size)
    return (jnp.cos(angle) + jnp.sin(angle)) / math.sqrt(grid_size)


def plane_freqs(total, box_size, planes):
    index = jnp.arange(total, dtype=jnp.int32)
    device = index // (2 * planes)
    offset = index % (2 * planes)
    low_freq = wrap_freq(device * planes + offset, box_size)
    high_freq = box_size // 2 + device * planes + offset - planes
    return jnp.where(offset < planes, low_freq, high_freq)


def square_freqs(box_size, first, planes):
    plane_f = wrap_freq(first + jnp.arange(planes, dtype=jnp.int32), box_size)
    inner = wrap_freq(jnp.arange(box_size, dtype=jnp.int32), box_size)
    total = plane_f[:, None, None] ** 2 + inner[None, :, None] ** 2 + inner[None, None, :] ** 2
    return (total.astype(jnp.float32) / float(box_size * box_size)).reshape(
        planes, box_size * box_size
    )


def negate_rows(square):
    return jnp.roll(jnp.flip(square, axis=-2), 1, axis=-2)


def negate_cols(square):
    return jnp.roll(jnp.flip(square, axis=-1), 1, axis=-1)


def all_turns(flat, box_size):
    square = flat.reshape(flat.shape[:-1] + (box_size, box_size))
    swapped = jnp.swapaxes(square, -1, -2)
    turned = [square, negate_rows(swapped), negate_rows(negate_cols(square)), negate_cols(swapped)]
    return [item.reshape(flat.shape) for item in turned]


def pick_turn(options, turns):
    picked = options[3]
    for which in (2, 1, 0):
        picked = jnp.where(turns == which, options[which], picked)
    return picked


def table_lookup(index, table):
    match = index[..., None] == jnp.arange(table.shape[0], dtype=jnp.int32)
    return jnp.sum(jnp.where(match, table, 0.0), axis=-1)


def extract_window(maps, planes, box_size):
    grid_size = maps.shape[2]
    half = box_size // 2
    lowest = maps[0, :planes]
    lowest = jnp.concatenate([lowest[:, :half], lowest[:, grid_size - half :]], axis=1)
    lowest = jnp.concatenate([lowest[:, :, :half], lowest[:, :, grid_size - half :]], axis=2)
    return lowest.reshape(planes, box_size * box_size)


def embed_window(cube, grid_size):
    planes, box_size = (cube.shape[0], cube.shape[1])
    half = box_size // 2
    middle = jnp.zeros((planes, grid_size - box_size, box_size), jnp.float32)
    rows_full = jnp.concatenate([cube[:, :half], middle, cube[:, half:]], axis=1)
    middle_cols = jnp.zeros((planes, grid_size, grid_size - box_size), jnp.float32)
    return jnp.concatenate([rows_full[:, :, :half], middle_cols, rows_full[:, :, half:]], axis=2)


def owner_terms(data, metas, window_turns, squares, defocus, tomo_gain):
    focus = table_lookup(metas[..., 0], defocus)
    gain = table_lookup(metas[..., 1], tomo_gain)
    turns = metas[..., 2]
    contrast = gain[..., None, None] * jnp.sin(focus[..., None, None] * squares + PHASE_SHIFT)
    turned = pick_turn(window_turns, turns[..., None, None])
    predicted = contrast * turned
    values = data.astype(jnp.float32)
    partial_value = jnp.sum(values * predicted, axis=(2, 3)) / BOX**1.5
    weighted = contrast * (predicted - values)
    back = pick_turn(all_turns(weighted, BOX), ((4 - turns) % 4)[..., None, None])
    return (partial_value, back)


def local(particles, class_list, orient, ctf_index, tomo_id, defocus, tomo_gain, maps):
    p_dev, planes = (particles.shape[0], particles.shape[1])
    n_map = lax.axis_size("map")
    n_dom = lax.axis_size("dom")
    first_plane = lax.axis_index("slab") * planes
    squares = square_freqs(BOX, first_plane, planes)
    window = extract_window(maps, planes, BOX)
    pair_count = p_dev * K
    pair_owner = jnp.repeat(jnp.arange(p_dev, dtype=jnp.int32), K)
    pair_class = class_list.reshape(-1)
    pair_turn = orient.reshape(-1)
    capacity = max(2, (pair_count + n_map - 1) // n_map)
    window_turns = all_turns(window, BOX)
    class_hot = (pair_class[:, None] == jnp.arange(n_map, dtype=jnp.int32)[None, :]).astype(
        jnp.int32
    )
    rank = jnp.sum((jnp.cumsum(class_hot, axis=0) - class_hot) * class_hot, axis=1)
    slot = pair_class * capacity + rank
    slot_hot = slot[:, None] == jnp.arange(n_map * capacity, dtype=jnp.int32)[None, :]
    pair_data = particles[pair_owner].reshape(pair_count, -1)
    send_data = jnp.dot(
        slot_hot.T.astype(jnp.bfloat16), pair_data, preferred_element_type=jnp.float32
    )
    send_data = send_data.astype(jnp.bfloat16).reshape(n_map, capacity, planes, -1)
    metas = jnp.stack([ctf_index[pair_owner], tomo_id[pair_owner] + 1, pair_turn], axis=1)
    send_meta = jnp.sum(jnp.where(slot_hot[:, :, None], metas[:, None, :], 0), axis=0)
    send_meta = send_meta.reshape(n_map, capacity, 3).at[..., 1].add(-1)
    data = lax.all_to_all(send_data, "map", split_axis=0, concat_axis=0, tiled=True)
    meta = lax.all_to_all(send_meta, "map", split_axis=0, concat_axis=0, tiled=True)
    partial_value, back = owner_terms(data, meta, window_turns, squares, defocus, tomo_gain)
    totals = lax.psum(partial_value, "slab")
    returned = lax.all_to_all(totals, "map", split_axis=0, concat_axis=0, tiled=True)
    back, returned = (back, returned)
    partial_sum = jnp.sum(back, axis=(0, 1))
    pair_scores = jnp.sum(jnp.where(slot_hot, returned.reshape(1, -1), 0.0), axis=1)
    data_grad = lax.psum(partial_sum, "dom") * (1.0 / (p_dev * n_dom * K))
    embedded = embed_window(data_grad.reshape(planes, BOX, BOX), L)
    scaled = TAU_REG * maps[0]
    grad = jnp.concatenate([scaled[:planes] + embedded, scaled[planes:]], axis=0)
    table = cas_table(jnp.arange(L, dtype=jnp.int32), L)
    first = jnp.einsum("quv,uy->qyv", grad, table, precision=lax.Precision.HIGHEST)
    second = jnp.einsum("qyv,vx->qyx", first, table, precision=lax.Precision.HIGHEST)
    pencil = lax.all_to_all(second, "slab", split_axis=1, concat_axis=0, tiled=True)
    plane_table = cas_table(plane_freqs(L, BOX, planes), L)
    real_grad = jnp.einsum("qyx,qz->zyx", pencil, plane_table, precision=lax.Precision.HIGHEST)
    return (real_grad[None], pair_scores.reshape(p_dev, K))


def solution(mesh):
    placed = (
        P(("dom", "map"), "slab", None),
        P(("dom", "map"), None),
        P(("dom", "map"), None),
        P(("dom", "map")),
        P(("dom", "map")),
        P(),
        P(),
        P("map", "slab", None, None),
    )
    return jax.shard_map(
        local,
        mesh=mesh,
        in_specs=placed,
        out_specs=(P("map", None, "slab", None), P(("dom", "map"), None)),
        check_vma=False,
    )
```

profile of v0, /device:TPU:1, one launch (start us, length us, event | category | flops | bytes accessed | tf_op | source)
XLA Modules:
  0.0 244.7 jit_solution(5163768308148400595)
XLA Ops:
  7.2 0.8 copy.113
  8.2 0.2 select_reduce_fusion.5
  8.5 1.3 gather_fusion.1
  9.9 1.4 gather_fusion
  11.2 0.8 copy.114
  12.3 0.7 copy.115
  13.0 17.2 %all-to-all-start = ((s32[8,2,3]{2,1,0:T(2,128)}), s32[8,2,3]{2,1,0:T(2,128)S(1)}, u32[]{:S(2)}, u32[]{:S(2)}) async-start(s32[8,2,3]{2,1,0:T(2,128)} %copy.115), calls=%async_computation | async-start | bytes 16384 | tf_op jit(solution)/shard_map/all_to_all | solution.py:133
  30.2 1.0 slice_bitcast_fusion.2
  31.3 0.1 slice_maximum_fusion
  32.2 0.1 reshape.328
  32.6 0.1 reshape.327
  32.9 0.1 reshape.329
  33.1 0.8 gather_fusion.2
  33.8 0.2 copy.142
  34.0 0.4 convolution_convert_fusion
  34.6 0.1 add.223
  34.9 0.1 reshape_reshape_reshape.3
  35.0 1.2 reshape.331
  36.2 0.6 pad.8.clone
  36.8 6.6 %all-to-all-start.1 = ((bf16[8,2,4,4096]{3,2,1,0:T(4,128)(2,1)}), bf16[8,2,4,4096]{3,2,1,0:T(4,128)(2,1)S(1)}, u32[]{:S(2)}, u32[]{:S(2)}) async-start(bf16[8,2,4,4096]{3,2,1,0:T(4,128)(2,1)} %reshape.331), calls=%async_computation.1 | async-start | bytes 1048576 | tf_op jit(solution)/shard_map/all_to_all | solution.py:132
  43.4 0.2 all-reduce.2.cloned.1.call-start
  44.2 0.2 select_reduce_fusion.3
  44.5 0.2 select_reduce_fusion.2
  44.8 0.7 copy.127
  45.5 0.7 copy.129
  46.2 0.6 copy.117
  46.8 13.0 %all-to-all-done.1 = bf16[8,2,4,4096]{3,2,1,0:T(4,128)(2,1)S(1)} async-done(((bf16[8,2,4,4096]{3,2,1,0:T(4,128)(2,1)}), bf16[8,2,4,4096]{3,2,1,0:T(4,128)(2,1)S(1)}, u32[]{:S(2)}, u32[]{:S(2)}) %all-to-all-start.1) | async-done | bytes 524320 | tf_op jit(solution)/shard_map/all_to_all | solution.py:132
  59.9 8.5 %fusion.1 = f32[8,2,4,4096]{3,2,1,0:T(4,128)} fusion(bf16[8,2,4,4096]{3,2,1,0:T(4,128)(2,1)S(1)} %all-to-all-done.1, f32[4,4096]{1,0:T(4,128)S(1)} %reshape.329, f32[4,4096]{1,0:T(4,128)S(1)} %reshape.328, f32[4,4096]{1,0:T(4,128)S(1)} %reshape.327, f32[4,4096]{1,0:T(4,128)S(1)} %reshape_reshape_reshape.3, f32[4,4096]{1,0:T(4,128)S(1)} %convert_multiply_fusion.1, ...), kind=kLoop, calls=%fused_computation.14 | loop fusion | flops 2621440 | bytes 1900720 | tf_op jit(solution)/shard_map/mul | solution.py:100
  68.4 2.1 reshape.332
  70.5 2.0 slice.229
  72.5 1.8 copy.128
  74.3 3.7 %slice.231 = f32[8,2,4,64,63]{4,3,2,1,0:T(8,128)} slice(f32[8,2,4,64,64]{4,3,2,1,0:T(8,128)} %bitcast.63), slice={[0:8], [0:2], [0:4], [0:64], [1:64]} | slice | bytes 2064384 | tf_op jit(solution)/shard_map/jit(_roll_static)/slice | solution.py:51
  78.0 1.6 slice.227
  79.6 0.6 slice.226
  80.3 4.2 %slice.188 = f32[8,2,4,64,63]{4,3,2,1,0:T(8,128)} reverse(f32[8,2,4,64,63]{4,3,2,1,0:T(8,128)} %slice.229), dimensions={4} | reverse | bytes 2064384 | tf_op jit(solution)/shard_map/jit(_roll_static)/slice | solution.py:51
  84.4 3.5 %pad_maximum_fusion = f32[8,2,4,63,64]{4,3,2,1,0:T(8,128)} fusion(f32[8,2,4,64,63]{4,3,2,1,0:T(8,128)} %slice.188, f32[8,2,4,64,1]{4,3,2,1,0:T(8,128)S(1)} %bitcast.61), kind=kLoop, calls=%fused_computation.4 | loop fusion | flops 258048 | bytes 2080768 | tf_op jit(solution)/shard_map/jit(_roll_static)/concatenate | solution.py:51
  88.0 3.9 %slice.191 = f32[8,2,4,63,64]{4,3,2,1,0:T(8,128)} reverse(f32[8,2,4,63,64]{4,3,2,1,0:T(8,128)} %pad_maximum_fusion), dimensions={3} | reverse | bytes 2064384 | tf_op jit(solution)/shard_map/jit(_roll_static)/slice | solution.py:47
  91.8 3.8 %fusion = f32[8,2,4,64,64]{4,3,2,1,0:T(8,128)} fusion(f32[8,2,4,64,63]{4,3,2,1,0:T(8,128)} %slice.188, f32[8,2,4,64,1]{4,3,2,1,0:T(8,128)S(1)} %bitcast.62, f32[8,2,4,63,64]{4,3,2,1,0:T(8,128)} %slice.191), kind=kLoop, calls=%fused_computation.6 | loop fusion | flops 1310720 | bytes 3129344 | tf_op jit(solution)/shard_map/jit(_roll_static)/concatenate | solution.py:47
  95.7 3.0 %reshape.334 = f32[8,2,4,4096]{3,2,1,0:T(4,128)} reshape(f32[8,2,4,64,64]{4,3,2,1,0:T(8,128)} %fusion) | data formatting | bytes 2097152 | tf_op jit(solution)/shard_map/reshape | solution.py:58
  98.7 4.3 %slice.194 = f32[8,2,4,64,63]{4,3,2,1,0:T(8,128)} reverse(f32[8,2,4,64,63]{4,3,2,1,0:T(8,128)} %slice.231), dimensions={4} | reverse | bytes 2064384 | tf_op jit(solution)/shard_map/jit(_roll_static)/slice | solution.py:51
  103.0 3.5 %pad_maximum_fusion.2 = f32[8,2,4,64,64]{4,3,2,1,0:T(8,128)} fusion(f32[8,2,4,64,63]{4,3,2,1,0:T(8,128)} %slice.194, f32[8,2,4,64,1]{4,3,2,1,0:T(8,128)S(1)} %bitcast.66), kind=kLoop, calls=%fused_computation.9 | loop fusion | flops 262144 | bytes 2097152 | tf_op jit(solution)/shard_map/jit(_roll_static)/concatenate | solution.py:51
  106.5 3.1 %reshape.335 = f32[8,2,4,4096]{3,2,1,0:T(4,128)} reshape(f32[8,2,4,64,64]{4,3,2,1,0:T(8,128)} %pad_maximum_fusion.2) | data formatting | bytes 2097152 | tf_op jit(solution)/shard_map/reshape | solution.py:58
  109.7 2.1 slice.185
  111.8 1.9 pad_maximum_fusion.1
  113.7 1.8 reshape.333
  115.6 11.0 %fusion.2 = (f32[8,2]{1,0:T(8,128)S(1)}, f32[4,4096]{1,0:T(4,128)}) fusion(bf16[8,2,4,4096]{3,2,1,0:T(4,128)(2,1)S(1)} %all-to-all-done.1, f32[4,4096]{1,0:T(4,128)} %copy-done.7, f32[4,4096]{1,0:T(4,128)} %copy-done.5, f32[4,4096]{1,0:T(4,128)} %copy-done.6, f32[4,4096]{1,0:T(4,128)} %copy-done.8, f32[4,4096]{1,0:T(4,128)} %copy-done.9, ...), kind=kLoop, calls=%fused_computation.15 | loop fusion | flops 4177904 | bytes 4063520 | tf_op jit(solution)/shard_map/reduce_sum | solution.py:99
  126.7 25.0 %psum.15 = f32[8,1,2]{0,2,1:T(2,128)S(1)} all-reduce(f32[8,1,2]{0,2,1:T(2,128)S(1)} %bitcast.73), channel_id=1, replica_groups=mesh['dom'=8,'map'=8,'slab'=16] {'slab'}, use_global_device_ids=true, to_apply=%region_8.9 | all-reduce | flops 16 | bytes 128 | tf_op jit(solution)/shard_map/psum | solution.py:135
  151.7 0.7 copy.134
  152.3 3.2 %all-to-all-start.3 = ((f32[8,1,2]{2,1,0:T(1,128)}), f32[8,1,2]{2,1,0:T(1,128)S(1)}, u32[]{:S(2)}, u32[]{:S(2)}) async-start(f32[8,1,2]{2,1,0:T(1,128)} %copy.134), calls=%async_computation.3 | async-start | bytes 8192 | tf_op jit(solution)/shard_map/all_to_all | solution.py:136
  155.6 46.9 %all-reduce.2.cloned.1.call-done = f32[4,4096]{1,0:T(4,128)} async-done(((f32[4,4096]{1,0:T(4,128)}), f32[4,4096]{1,0:T(4,128)}) %all-reduce.2.cloned.1.call-update) | async-done | bytes 65552 | tf_op jit(solution)/shard_map/psum | solution.py:140
  202.5 0.9 broadcast_multiply_fusion.1
  203.4 0.1 reshape.336
  203.6 0.1 fusion.66
  203.8 0.1 fusion.10
  203.9 0.9 convolution_bitcast_fusion.1
  204.8 1.8 fusion.7
  206.6 11.9 %all-to-all-start.2 = ((f32[8,128,128]{2,0,1:T(8,128)}), f32[8,128,128]{2,0,1:T(8,128)S(1)}, u32[]{:S(2)}, u32[]{:S(2)}) async-start(f32[8,128,128]{2,0,1:T(8,128)} %fusion.7), calls=%async_computation.2 | async-start | bytes 1048576 | tf_op jit(solution)/shard_map/all_to_all | solution.py:147
  218.6 0.5 broadcast.496
  219.1 0.7 reduce.5
  219.8 0.2 select_reduce_fusion.4
  220.1 0.7 copy.136
  220.7 15.1 %all-to-all-done.2 = f32[8,128,128]{2,0,1:T(8,128)S(1)} async-done(((f32[8,128,128]{2,0,1:T(8,128)}), f32[8,128,128]{2,0,1:T(8,128)S(1)}, u32[]{:S(2)}, u32[]{:S(2)}) %all-to-all-start.2) | async-done | bytes 524320 | tf_op jit(solution)/shard_map/all_to_all | solution.py:147
  235.9 0.9 convolution_bitcast_fusion
  236.7 1.1 copy.135
  (98 shorter events, 3.4 us)
Async XLA Ops:
  7.2 25.9 %copy-start = (bf16[4,4,4096]{2,1,0:T(4,128)(2,1)S(1)}, bf16[4,4,4096]{2,1,0:T(4,128)(2,1)}, u32[]{:S(2)}) copy-start(bf16[4,4,4096]{2,1,0:T(4,128)(2,1)} %param.10) | copy-start | bytes 393220
  8.4 25.6 %copy-start.14 = (s32[8]{0:T(128)}, s32[8]{0:T(128)S(1)}, u32[]{:S(2)}) copy-start(s32[8]{0:T(128)S(1)} %multiply_add_fusion) | copy-start | bytes 100
  9.9 22.2 %copy-start.4 = (f32[1,8,128,128]{3,2,1,0:T(8,128)S(1)}, f32[1,8,128,128]{3,2,1,0:T(8,128)}, u32[]{:S(2)}) copy-start(f32[1,8,128,128]{3,2,1,0:T(8,128)} %param.17) | copy-start | bytes 1572868
  13.0 23.8 %all-to-all-start = ((s32[8,2,3]{2,1,0:T(2,128)}), s32[8,2,3]{2,1,0:T(2,128)S(1)}, u32[]{:S(2)}, u32[]{:S(2)}) async-start(s32[8,2,3]{2,1,0:T(2,128)} %copy.115), calls=%async_computation | async-start | bytes 16384 | tf_op jit(solution)/shard_map/all_to_all | solution.py:133
  32.3 27.5 %copy-start.5 = (f32[4,4096]{1,0:T(4,128)}, f32[4,4096]{1,0:T(4,128)S(1)}, u32[]{:S(2)}) copy-start(f32[4,4096]{1,0:T(4,128)S(1)} %reshape.328) | copy-start | bytes 196612
  32.7 27.1 %copy-start.6 = (f32[4,4096]{1,0:T(4,128)}, f32[4,4096]{1,0:T(4,128)S(1)}, u32[]{:S(2)}) copy-start(f32[4,4096]{1,0:T(4,128)S(1)} %reshape.327) | copy-start | bytes 196612
  33.1 26.8 %copy-start.7 = (f32[4,4096]{1,0:T(4,128)}, f32[4,4096]{1,0:T(4,128)S(1)}, u32[]{:S(2)}) copy-start(f32[4,4096]{1,0:T(4,128)S(1)} %reshape.329) | copy-start | bytes 196612
  34.0 10.2 %copy-start.12 = (f32[32]{0:T(128)S(1)}, f32[32]{0:T(128)}, u32[]{:S(2)}) copy-start(f32[32]{0:T(128)} %param.16) | copy-start | bytes 388
  34.0 10.5 %copy-start.13 = (f32[64]{0:T(128)S(1)}, f32[64]{0:T(128)}, u32[]{:S(2)}) copy-start(f32[64]{0:T(128)} %param.15) | copy-start | bytes 772
  34.9 25.0 %copy-start.9 = (f32[4,4096]{1,0:T(4,128)}, f32[4,4096]{1,0:T(4,128)S(1)}, u32[]{:S(2)}) copy-start(f32[4,4096]{1,0:T(4,128)S(1)} %convert_multiply_fusion.1) | copy-start | bytes 196612
  35.0 24.8 %copy-start.8 = (f32[4,4096]{1,0:T(4,128)}, f32[4,4096]{1,0:T(4,128)S(1)}, u32[]{:S(2)}) copy-start(f32[4,4096]{1,0:T(4,128)S(1)} %reshape_reshape_reshape.3) | copy-start | bytes 196612
  36.8 23.0 %all-to-all-start.1 = ((bf16[8,2,4,4096]{3,2,1,0:T(4,128)(2,1)}), bf16[8,2,4,4096]{3,2,1,0:T(4,128)(2,1)S(1)}, u32[]{:S(2)}, u32[]{:S(2)}) async-start(bf16[8,2,4,4096]{3,2,1,0:T(4,128)(2,1)} %reshape.331), calls=%async_computation.1 | async-start | bytes 1048576 | tf_op jit(solution)/shard_map/all_to_all | solution.py:132
  43.4 159.1 %all-reduce.2.cloned.1.call-start = ((), (), s32[]{:S(2)}) async-start(), calls=%async_computation.4 | async-start | bytes 131072 | tf_op jit(solution)/shard_map/psum | solution.py:140
  44.1 15.7 %copy-start.10 = (pred[8,2]{1,0:T(8,128)(4,1)}, pred[8,2]{1,0:T(8,128)(4,1)S(1)}, u32[]{:S(2)}) copy-start(pred[8,2]{1,0:T(8,128)(4,1)S(1)} %copy.125) | copy-start | bytes 52
  74.3 3.7 %copy-start.1 = (f32[8,2,4,64,64]{3,4,2,1,0:T(8,128)S(1)}, f32[8,2,4,64,64]{3,4,2,1,0:T(8,128)}, u32[]{:S(2)}) copy-start(f32[8,2,4,64,64]{3,4,2,1,0:T(8,128)} %copy.128) | copy-start | bytes 3145732
  98.7 4.3 %copy-start.2 = (f32[8,2,4,64,64]{3,4,2,1,0:T(8,128)S(1)}, f32[8,2,4,64,64]{3,4,2,1,0:T(8,128)}, u32[]{:S(2)}) copy-start(f32[8,2,4,64,64]{3,4,2,1,0:T(8,128)} %copy.128) | copy-start | bytes 3145732
  106.5 3.1 %copy-start.3 = (f32[8,2,4,63,64]{4,3,2,1,0:T(8,128)S(1)}, f32[8,2,4,63,64]{4,3,2,1,0:T(8,128)}, u32[]{:S(2)}) copy-start(f32[8,2,4,63,64]{4,3,2,1,0:T(8,128)} %slice.227) | copy-start | bytes 3096580
  115.6 88.0 %copy-start.11 = (f32[128]{0:T(128)S(1)}, f32[128]{0:T(128)}, u32[]{:S(2)}) copy-start(f32[128]{0:T(128)} %pad.8.clone) | copy-start | bytes 1540
  152.3 54.3 %all-to-all-start.3 = ((f32[8,1,2]{2,1,0:T(1,128)}), f32[8,1,2]{2,1,0:T(1,128)S(1)}, u32[]{:S(2)}, u32[]{:S(2)}) async-start(f32[8,1,2]{2,1,0:T(1,128)} %copy.134), calls=%async_computation.3 | async-start | bytes 8192 | tf_op jit(solution)/shard_map/all_to_all | solution.py:136
  203.8 16.1 %copy-start.15 = (s32[8]{0:T(128)S(1)}, s32[8]{0:T(128)}, u32[]{:S(2)}) copy-start(s32[8]{0:T(128)} %copy-done.14) | copy-start | bytes 100
  206.6 29.2 %all-to-all-start.2 = ((f32[8,128,128]{2,0,1:T(8,128)}), f32[8,128,128]{2,0,1:T(8,128)S(1)}, u32[]{:S(2)}, u32[]{:S(2)}) async-start(f32[8,128,128]{2,0,1:T(8,128)} %fusion.7), calls=%async_computation.2 | async-start | bytes 1048576 | tf_op jit(solution)/shard_map/all_to_all | solution.py:147
Sparse Core Ops, SparseCore 0:
  126.7 75.7 all-reduce.1
where the time goes:
time: 246 us; the launch traced here: 245 us
  waiting for transfers between devices  75.2 us (31%)
  local copies, waits for them, and re-layouts  50.9 us (21%)
  starting transfers between devices  39.2 us (16%)
  other arithmetic  36 us (15%)
  blocking collectives  25 us (10%)
  between operations  14.5 us (6%)
  matrix products  3.99 us (2%)
    psum x1, waiting for transfers between devices, local(): data_grad = lax.psum(partial_sum, 'dom') * (1.0 / (p_dev * n_dom * K))  46.9 us
    psum x1, blocking collectives, local(): totals = lax.psum(partial_value, 'slab')  25 us
    all_to_all x1, starting transfers between devices, local(): lax.all_to_all(send_meta, 'map', split_axis=0, concat_axis=0, tiled=True)  17.2 us
    all_to_all x1, waiting for transfers between devices, local(): lax.all_to_all(second, 'slab', split_axis=1, concat_axis=0, tiled=True)  15.1 us
    slice x8, local copies, waits for them, and re-layouts, negate_cols(): return jnp.roll(jnp.flip(square, axis=-1), 1, axis=-1)  14.3 us
    all_to_all x1, waiting for transfers between devices, local(): lax.all_to_all(send_data, 'map', split_axis=0, concat_axis=0, tiled=True)  13 us
    all_to_all x1, starting transfers between devices, local(): lax.all_to_all(second, 'slab', split_axis=1, concat_axis=0, tiled=True)  11.9 us
    reduce_sum x1, other arithmetic, owner_terms(): partial_value = jnp.sum(values * predicted, axis=(2, 3)) / BOX ** 1.5  11 us
  transfers between devices with their start and end apart: 5, of which 3 were waited for; matrix products, arithmetic and copies ran while one was open for 7% of the time, Pallas kernels for 0%

commit v1 on v0

v1 whole, which is shorter than its diff:
```python
import functools
import math

import jax
import jax.numpy as jnp
import numpy as np
from jax import lax
from jax.experimental import pallas as pl
from jax.experimental.pallas import tpu as pltpu
from jax.sharding import PartitionSpec as P

L = 128
BOX = 64
K = 2
P_DEV = 4
PLANES = 4
TAU_REG = 0.1
PHASE_SHIFT = 0.1
F32 = jnp.float32
BF16 = jnp.bfloat16


def ring_order(n):
    order = []
    for step in range(1, n // 2 + 1):
        order += [step] if 2 * step == n else [step, n - step]
    return order


def wrap(index, size):
    return jnp.where(index < size // 2, index, index - size)


def fast_sin(x):
    turns = jnp.floor(x * (1.0 / math.pi) + 0.5)
    r = x - turns * 3.140625
    r = r - turns * 9.67653589793e-4
    odd = turns - 2.0 * jnp.floor(turns * 0.5)
    r = r * (1.0 - 2.0 * odd)
    s = r * r
    poly = -1.0 / 39916800.0
    for c in (1.0 / 362880.0, -1.0 / 5040.0, 1.0 / 120.0, -1.0 / 6.0):
        poly = poly * s + c
    return r + r * s * poly


def split(x):
    high = x.astype(BF16)
    return high, (x - high.astype(F32)).astype(BF16)


def dot(a, b):
    return jnp.dot(a, b, preferred_element_type=F32)


def dot3(a, b):
    return dot(a[0], b[0]) + (dot(a[0], b[1]) + dot(a[1], b[0]))


def tables(n_slab):
    def cas(rows, cols):
        angle = (np.outer(rows, cols) % L) * (2.0 * math.pi / L)
        return (np.cos(angle) + np.sin(angle)) / math.sqrt(L)

    points = np.arange(L)
    wrapped = np.where(np.arange(BOX) < BOX // 2, np.arange(BOX), np.arange(BOX) - BOX)
    rows = cas(points, points)
    window = cas(wrapped, points)
    q = np.arange(2 * PLANES * n_slab)
    s, r = q // (2 * PLANES), q % (2 * PLANES)
    low = s * PLANES + r
    low = np.where(low < BOX // 2, low, low - BOX)
    freq = np.where(r < PLANES, low, BOX // 2 + s * PLANES + r - PLANES)
    planes = cas(points, freq)
    full = np.zeros((L, L))
    full[:, : len(q)] = planes
    picked = np.zeros((L, L))
    half = 2 * n_slab
    for jj in range(2):
        for row in range(half):
            picked[:, jj * half + row] = planes[:, (row // 2) * 2 * PLANES + 2 * (row % 2) + jj]
    none = np.zeros((BOX, L))
    negate = np.zeros((L, L))
    for block in range(2):
        for a in range(BOX):
            negate[block * BOX + a, block * BOX + (-a) % BOX] = 1.0
    first = np.concatenate([window.T, window.T], axis=1) / 64.0
    mats = [
        rows * TAU_REG,
        rows,
        full,
        picked,
        first,
        np.concatenate([window, none]),
        np.concatenate([none, window]),
        negate,
    ]
    pairs = []
    for mat in mats:
        mat = mat.astype(np.float32)
        high = mat.astype(jnp.bfloat16)
        pairs += [high, (mat - high.astype(np.float32)).astype(jnp.bfloat16)]
    return np.stack(pairs)


def kernel(
    sizes,
    part,
    cls,
    ori,
    cidx,
    tid,
    focus,
    gain,
    maps,
    tab,
    out,
    score_out,
    tmp,
    xs,
    send_a,
    recv_a,
    send_m,
    recv_m,
    send1,
    recv1,
    acc,
    wrot,
    ctf,
    sums,
    sc_send,
    sc_recv,
    ss_send,
    ss_recv,
    dbuf,
    rs_recv,
    red,
    dfull,
    send2,
    recv2,
    vbuf,
    m_s,
    m_r,
    a_s,
    a_r,
    c1_s,
    c1_r,
    sc_s,
    sc_r,
    ss_s,
    ss_r,
    rs_s,
    rs_r,
    ag_s,
    ag_r,
    c2_s,
    c2_r,
):
    n_dom, n_map, n_slab = sizes
    rows = L // n_slab
    chunk = L // n_dom
    d, m, s = lax.axis_index("dom"), lax.axis_index("map"), lax.axis_index("slab")
    axes = {"dom": (d, n_dom), "map": (m, n_map), "slab": (s, n_slab)}

    def ahead(axis, step):
        me, n = axes[axis]
        return lax.rem(me + step, n)

    def remote(axis, step, src, dst, ssem, rsem):
        return pltpu.make_async_remote_copy(
            src_ref=src,
            dst_ref=dst,
            send_sem=ssem.at[step],
            recv_sem=rsem.at[step],
            device_id={axis: ahead(axis, step)},
            device_id_type=pl.DeviceIdType.MESH,
        )

    barrier = pltpu.get_barrier_semaphore()
    for axis, (_, n) in axes.items():
        for step in range(1, n):
            pl.semaphore_signal(
                barrier,
                inc=1,
                device_id={axis: ahead(axis, step)},
                device_id_type=pl.DeviceIdType.MESH,
            )

    lane = lax.broadcasted_iota(jnp.int32, (L, L), 1)
    row = lax.broadcasted_iota(jnp.int32, (L, L), 0)
    lane8 = lax.broadcasted_iota(jnp.int32, (8, L), 1)
    row8 = lax.broadcasted_iota(jnp.int32, (8, L), 0)

    for g in range(2):
        both = jnp.concatenate([part[2 * g].astype(F32), part[2 * g + 1].astype(F32)], axis=0)
        up = pltpu.roll(both, 7, 0)
        for k in range(BOX // 2):
            here, above = both[:, k * L : (k + 1) * L], up[:, k * L : (k + 1) * L]
            even = jnp.where(lane8 < BOX, here, pltpu.roll(above, BOX, 1))
            odd = jnp.where(lane8 < BOX, pltpu.roll(here, BOX, 1), above)
            tmp[k] = jnp.where(row8 % 2 == 0, even, pltpu.roll(odd, 1, 0))
        for i in range(4):
            for h in range(2):
                start = (i % 2) * BOX + h
                xs[2 * g + i // 2, pl.ds(start, BOX // 2, stride=2), :] = tmp[:, 2 * i + h, :]

    def build(c, carry):
        found = jnp.int32(0)
        who = [jnp.int32(0)] * 2
        turn = [jnp.int32(0)] * 2
        for p in range(P_DEV):
            for i in range(K):
                hit = cls[i, p] == c
                for k in range(2):
                    mine = jnp.logical_and(hit, found == k)
                    who[k] = jnp.where(mine, p, who[k])
                    turn[k] = jnp.where(mine, ori[i, p], turn[k])
                found = found + hit.astype(jnp.int32)
        meta = jnp.zeros((8, L), F32)
        for k in range(2):
            power = jnp.where(found > k, gain[tid[who[k]]], 0.0)
            meta = jnp.where(row8 == 4 * k, focus[cidx[who[k]]], meta)
            meta = jnp.where(row8 == 4 * k + 1, power, meta)
            meta = jnp.where(row8 == 4 * k + 2, turn[k].astype(F32), meta)
            send_a[c, k * L : (k + 1) * L, :] = xs[who[k]].astype(BF16)
        send_m[c] = meta
        return carry

    lax.fori_loop(0, n_map, build, 0)

    pl.semaphore_wait(barrier, n_dom + n_map + n_slab - 3)

    map_order = ring_order(n_map)
    dom_order = ring_order(n_dom)
    slab_order = ring_order(n_slab)

    def meta_copy(step):
        return remote("map", step, send_m.at[ahead("map", step)], recv_m.at[m], m_s, m_r)

    def data_copy(step):
        return remote("map", step, send_a.at[ahead("map", step)], recv_a.at[m], a_s, a_r)

    for step in map_order:
        meta_copy(step).start()
    for step in map_order:
        data_copy(step).start()

    def table(i):
        return tab[2 * i], tab[2 * i + 1]

    for q in range(2 * PLANES):
        across = dot3(split(maps[0, q]), table(0))
        send1[:, q, :] = dot3(table(1), split(across))

    def first_copy(step):
        return remote(
            "slab",
            step,
            send1.at[pl.ds(ahead("slab", step) * rows, rows)],
            recv1.at[:, pl.ds(s * 2 * PLANES, 2 * PLANES), :],
            c1_s,
            c1_r,
        )

    for step in slab_order:
        first_copy(step).start()
    recv1[:, pl.ds(s * 2 * PLANES, 2 * PLANES), :] = send1[pl.ds(s * rows, rows)]

    negate = tab[14]

    def by_left(x):
        high, low = split(x)
        return dot(negate, high) + dot(negate, low)

    def by_right(x):
        high, low = split(x)
        return dot(high, negate) + dot(low, negate)

    def swapped(x):
        t = x.T
        other = pltpu.roll(pltpu.roll(t, BOX, 0), BOX, 1)
        return jnp.where(row // BOX == lane // BOX, t, other)

    halves = []
    for jp in range(2):
        cut = []
        for jj in range(2):
            plane = maps[0, 2 * jp + jj]
            cut.append(jnp.concatenate([plane[: BOX // 2], plane[L - BOX // 2 :]], axis=0))
        lane64 = lane[:BOX]
        first = jnp.where(lane64 < BOX // 2, cut[0], pltpu.roll(cut[0], BOX, 1))
        second = jnp.where(lane64 < L - BOX // 2, pltpu.roll(cut[1], BOX, 1), cut[1])
        halves.append(jnp.where(lane64 < BOX, first, second))
    window = jnp.concatenate(halves, axis=0)
    window_n = by_right(window)
    wrot[0] = window
    wrot[1] = swapped(window_n)
    wrot[2] = by_left(window_n)
    wrot[3] = swapped(by_left(window))

    fj = wrap(s * PLANES + 2 * (row // BOX) + lane // BOX, BOX)
    fa, fb = wrap(row % BOX, BOX), wrap(lane % BOX, BOX)
    squares = (fj * fj + fa * fa + fb * fb).astype(F32) * (1.0 / (BOX * BOX))

    def contrast(meta, src, total):
        for k in range(2):
            value = meta[4 * k + 1 : 4 * k + 2] * fast_sin(meta[4 * k : 4 * k + 1] * squares + PHASE_SHIFT)
            ctf[src, k] = value
            total = total + value * value
        return total

    power = contrast(send_m[m], m, jnp.zeros((L, L), F32))
    for step in map_order:
        meta_copy(step).wait_recv()
    power = lax.fori_loop(
        1,
        n_map,
        lambda step, total: contrast(recv_m[lax.rem(m + step, n_map)], lax.rem(m + step, n_map), total),
        power,
    )
    dbuf[...] = wrot[0] * power

    sums[...] = jnp.zeros_like(sums)

    def collect(data, meta, src):
        lines = jnp.zeros((8, L), F32)
        for k in range(2):
            z = data[k * L : (k + 1) * L].astype(F32) * ctf[src, k]
            turn = meta[4 * k + 2 : 4 * k + 3]
            found = jnp.zeros((L, L), F32)
            for o in range(4):
                part_o = jnp.where(turn == float(o), z, 0.0)
                sums[o] += part_o
                found = found + part_o * wrot[o]
            lines = jnp.where(row8 == k, jnp.sum(found, axis=0, keepdims=True), lines)
        return lines * (1.0 / BOX**1.5)

    sc_recv[m] = collect(send_a[m], send_m[m], m)
    for step in map_order:
        src = lax.rem(m + n_map - step, n_map)
        remote("map", step, send_a.at[src], recv_a.at[src], a_s, a_r).wait_recv()
        sc_send[src] = collect(recv_a[src], recv_m[src], src)

    def score_copy(step):
        return remote("map", step, sc_send.at[ahead("map", step)], sc_recv.at[m], sc_s, sc_r)

    turned = swapped(by_left(sums[1]) + by_right(sums[3]))
    dbuf[...] = dbuf[...] - (sums[0] + by_left(by_right(sums[2])) + turned)

    def scatter_copy(step):
        return remote("dom", step, dbuf.at[pl.ds(ahead("dom", step) * chunk, chunk)], rs_recv.at[d], rs_s, rs_r)

    for step in dom_order:
        scatter_copy(step).start()
    for step in map_order:
        score_copy(step).start()
    rs_recv[d] = dbuf[pl.ds(d * chunk, chunk)]
    for step in dom_order:
        src = lax.rem(d + n_dom - step, n_dom)
        remote("dom", step, dbuf.at[pl.ds(0, chunk)], rs_recv.at[src], rs_s, rs_r).wait_recv()
    total = rs_recv[0]
    for i in range(1, n_dom):
        total = total + rs_recv[i]
    red[...] = total

    def gather_copy(step):
        return remote("dom", step, red, dfull.at[pl.ds(d * chunk, chunk)], ag_s, ag_r)

    for step in dom_order:
        gather_copy(step).start()
    dfull[pl.ds(d * chunk, chunk)] = total

    for step in map_order:
        src = lax.rem(m + n_map - step, n_map)
        remote("map", step, sc_send.at[src], sc_recv.at[src], sc_s, sc_r).wait_recv()
    flat = [jnp.sum(sc_recv[:, k, :], axis=1, keepdims=True) for k in range(2)]
    lane_m = lax.broadcasted_iota(jnp.int32, (n_map, L), 1)
    ss_send[...] = jnp.where(lane_m == 0, flat[0], jnp.where(lane_m == 1, flat[1], 0.0))

    def spread_copy(step):
        return remote("slab", step, ss_send, ss_recv.at[s], ss_s, ss_r)

    for step in slab_order:
        spread_copy(step).start()
    ss_recv[s] = ss_send[...]

    for step in dom_order:
        src = lax.rem(d + n_dom - step, n_dom)
        remote("dom", step, red, dfull.at[pl.ds(src * chunk, chunk)], ag_s, ag_r).wait_recv()

    for jp in range(2):
        columns = dot3(
            (tab[8][:, :BOX], tab[9][:, :BOX]), split(dfull[jp * BOX : (jp + 1) * BOX])
        )
        send2[:, jp] = columns.reshape(n_slab, rows, L)

    def second_copy(step):
        return remote("slab", step, send2.at[ahead("slab", step)], recv2.at[s], c2_s, c2_r)

    for step in slab_order:
        second_copy(step).start()
    recv2[s] = send2[s]

    for step in slab_order:
        src = lax.rem(s + n_slab - step, n_slab)
        remote(
            "slab",
            step,
            send1.at[pl.ds(0, rows)],
            recv1.at[:, pl.ds(src * 2 * PLANES, 2 * PLANES), :],
            c1_s,
            c1_r,
        ).wait_recv()
    deep = 2 * PLANES * n_slab
    by_plane = (tab[4][:, :deep], tab[5][:, :deep])
    for y in range(rows):
        acc[y] = dot3(by_plane, split(recv1[y]))

    for step in slab_order:
        src = lax.rem(s + n_slab - step, n_slab)
        remote("slab", step, ss_send, ss_recv.at[src], ss_s, ss_r).wait_recv()
    tally = ss_recv[0]
    for i in range(1, n_slab):
        tally = tally + ss_recv[i]
    row_m = lax.broadcasted_iota(jnp.int32, (n_map, L), 0)
    out_row = lax.broadcasted_iota(jnp.int32, (K, P_DEV), 0)
    out_col = lax.broadcasted_iota(jnp.int32, (K, P_DEV), 1)
    found = jnp.zeros((K, P_DEV), F32)
    for p in range(P_DEV):
        for i in range(K):
            c = cls[i, p]
            rank = jnp.int32(0)
            for e in range(p * K + i):
                rank = rank + (cls[e % K, e // K] == c).astype(jnp.int32)
            here = jnp.logical_and(row_m == c, lane_m == rank)
            one = jnp.sum(jnp.where(here, tally, 0.0), axis=0, keepdims=True)
            one = jnp.sum(one, axis=1, keepdims=True)
            found = jnp.where(jnp.logical_and(out_row == i, out_col == p), one, found)
    score_out[...] = found

    for step in slab_order:
        src = lax.rem(s + n_slab - step, n_slab)
        remote("slab", step, send2.at[0], recv2.at[src], c2_s, c2_r).wait_recv()
    lines = split(recv2[...].reshape(n_slab * 2 * rows, L))
    half = 2 * n_slab
    for jj in range(2):
        vbuf[jj * half : (jj + 1) * half] = dot3(lines, table(5 + jj)).reshape(half, rows, L)
    by_low = (tab[6][:, : 2 * half], tab[7][:, : 2 * half])
    for y in range(rows):
        out[0, :, y, :] = acc[y] + dot3(by_low, split(vbuf[:, y, :]))

    for step in map_order:
        meta_copy(step).wait_send()
        data_copy(step).wait_send()
        score_copy(step).wait_send()
    for step in dom_order:
        scatter_copy(step).wait_send()
        gather_copy(step).wait_send()
    for step in slab_order:
        first_copy(step).wait_send()
        spread_copy(step).wait_send()
        second_copy(step).wait_send()


def solution(mesh):
    n_dom, n_map, n_slab = (mesh.shape[a] for a in ("dom", "map", "slab"))
    rows, chunk = L // n_slab, L // n_dom
    tab = tables(n_slab)
    vmem = pl.BlockSpec(memory_space=pltpu.VMEM)
    smem = pl.BlockSpec(memory_space=pltpu.SMEM)
    dma = pltpu.SemaphoreType.DMA

    def local(particles, class_list, orient, ctf_index, tomo_id, defocus, tomo_gain, maps):
        real_grad, scores = pl.pallas_call(
            functools.partial(kernel, (n_dom, n_map, n_slab)),
            out_shape=(
                jax.ShapeDtypeStruct((1, L, rows, L), F32),
                jax.ShapeDtypeStruct((K, P_DEV), F32),
            ),
            in_specs=[vmem] + [smem] * 6 + [vmem] * 2,
            out_specs=(vmem, vmem),
            scratch_shapes=[
                pltpu.VMEM((BOX // 2, 8, L), F32),
                pltpu.VMEM((P_DEV, L, L), F32),
                pltpu.VMEM((n_map, 2 * L, L), BF16),
                pltpu.VMEM((n_map, 2 * L, L), BF16),
                pltpu.VMEM((n_map, 8, L), F32),
                pltpu.VMEM((n_map, 8, L), F32),
                pltpu.VMEM((L, 2 * PLANES, L), F32),
                pltpu.VMEM((rows, 2 * PLANES * n_slab, L), F32),
                pltpu.VMEM((rows, L, L), F32),
                pltpu.VMEM((4, L, L), F32),
                pltpu.VMEM((n_map, 2, L, L), F32),
                pltpu.VMEM((4, L, L), F32),
                pltpu.VMEM((n_map, 8, L), F32),
                pltpu.VMEM((n_map, 8, L), F32),
                pltpu.VMEM((n_map, L), F32),
                pltpu.VMEM((n_slab, n_map, L), F32),
                pltpu.VMEM((L, L), F32),
                pltpu.VMEM((n_dom, chunk, L), F32),
                pltpu.VMEM((chunk, L), F32),
                pltpu.VMEM((L, L), F32),
                pltpu.VMEM((n_slab, 2, rows, L), F32),
                pltpu.VMEM((n_slab, 2, rows, L), F32),
                pltpu.VMEM((4 * n_slab, rows, L), F32),
            ]
            + [dma((n_map,))] * 4
            + [dma((n_slab,))] * 2
            + [dma((n_map,))] * 2
            + [dma((n_slab,))] * 2
            + [dma((n_dom,))] * 4
            + [dma((n_slab,))] * 2,
            compiler_params=pltpu.CompilerParams(
                collective_id=0, has_side_effects=True, vmem_limit_bytes=48 * 2**20
            ),
        )(particles, class_list.T, orient.T, ctf_index, tomo_id, defocus, tomo_gain, maps, tab)
        return real_grad, scores.T

    pair = P(("dom", "map"))
    return jax.shard_map(
        local,
        mesh=mesh,
        in_specs=(
            P(("dom", "map"), "slab", None),
            pair,
            pair,
            pair,
            pair,
            P(),
            P(),
            P("map", "slab", None, None),
        ),
        out_specs=(P("map", None, "slab", None), pair),
        check_vma=False,
    )
```

time: 246 us -> 62.3 us (0.25)
  waiting for transfers between devices: 75.2 us -> 0 us
  Pallas kernels: 0 us -> 55.6 us
  local copies, waits for them, and re-layouts: 50.9 us -> 5.69 us
  starting transfers between devices: 39.2 us -> 0 us
  other arithmetic: 36 us -> 0 us
  blocking collectives: 25 us -> 0 us
  between operations: 14.5 us -> 0.69 us
  matrix products: 3.99 us -> 0 us
    pallas_call x0 -> x1, Pallas kernels: none -> 55.6 us  [local(): pl.pallas_call(functools.partial(kernel, (n_dom, n_map, n_slab)), out_sha...]
    psum x1 -> x0, waiting for transfers between devices: 46.9 us -> none  [local(): data_grad = lax.psum(partial_sum, 'dom') * (1.0 / (p_dev * n_dom * K))]
    all_to_all x4 -> x0, starting transfers between devices: 39 us -> none  [the longest x1 17.2 us: local(): lax.all_to_all(send_meta, 'map', split_axis=0, concat_axis=0, tiled=True)]
    all_to_all x4 -> x0, waiting for transfers between devices: 28.2 us -> none  [the longest x1 15.1 us: local(): lax.all_to_all(second, 'slab', split_axis=1, concat_axis=0, tiled=True)]
    psum x1 -> x0, blocking collectives: 25 us -> none  [local(): totals = lax.psum(partial_value, 'slab')]
    slice x24 -> x0, local copies, waits for them, and re-layouts: 23.2 us -> none  [the longest x8 14.3 us: negate_cols(): return jnp.roll(jnp.flip(square, axis=-1), 1, axis=-1)]
    reshape x14 -> x0, local copies, waits for them, and re-layouts: 13.9 us -> none  [the longest x6 8.34 us: all_turns(): return [item.reshape(flat.shape) for item in turned]]
    concatenate x12 -> x0, other arithmetic: 13.5 us -> none  [the longest x4 7.16 us: negate_cols(): return jnp.roll(jnp.flip(square, axis=-1), 1, axis=-1)]
  transfers between devices with their start and end apart: 5 -> 0, of which waited for: 3 -> 0; matrix products, arithmetic and copies ran while one was open for 7% -> 0% of each run, Pallas kernels for 0% -> 0%
where the time goes in v1:
time: 62.3 us; the launch traced here: 62 us
  Pallas kernels  55.6 us (89%)
  local copies, waits for them, and re-layouts  5.69 us (9%)
  between operations  0.69 us (1%)
    pallas_call x1, Pallas kernels, local(): pl.pallas_call(functools.partial(kernel, (n_dom, n_map, n_slab)), out_sha...  55.6 us
    unnamed x20, local copies, waits for them, and re-layouts  5.69 us

profile of v1, /device:TPU:1, one launch (start us, length us, event | category | flops | bytes accessed | tf_op | source)
XLA Modules:
  0.0 62.0 jit_solution(14467637861960697103)
XLA Ops:
  0.6 0.0 copy-start.4
  0.6 0.0 copy-start.6
  0.7 0.0 copy-start.7
  0.7 0.0 copy-start.3
  0.7 0.0 copy-start.5
  0.7 0.6 %copy-done.4 = s32[4,2]{0,1:T(2,128)S(1)} copy-done((s32[4,2]{0,1:T(2,128)S(1)}, s32[4,2]{0,1:T(2,128)}, u32[]{:S(2)}) %copy-start.4) | copy-done | bytes 56
  1.3 0.0 copy-done.6
  1.3 0.0 copy-done.7
  1.3 0.0 copy-done.3
  1.4 0.0 copy-done.5
  1.4 0.0 copy-start
  1.4 1.0 %copy-done = f32[1,8,128,128]{3,2,1,0:T(8,128)S(1)} copy-done((f32[1,8,128,128]{3,2,1,0:T(8,128)S(1)}, f32[1,8,128,128]{3,2,1,0:T(8,128)}, u32[]{:S(2)}) %copy-start) | copy-done | bytes 524312
  2.4 0.0 copy-start.1
  2.4 1.0 %copy-done.1 = bf16[16,128,128]{2,1,0:T(8,128)(2,1)S(1)} copy-done((bf16[16,128,128]{2,1,0:T(8,128)(2,1)S(1)}, bf16[16,128,128]{2,1,0:T(8,128)(2,1)}, u32[]{:S(2)}) %copy-start.1) | copy-done | bytes 524312
  3.4 0.0 copy-start.2
  3.4 0.9 %copy-done.2 = bf16[4,4,4096]{2,1,0:T(4,128)(2,1)S(1)} copy-done((bf16[4,4,4096]{2,1,0:T(4,128)(2,1)S(1)}, bf16[4,4,4096]{2,1,0:T(4,128)(2,1)}, u32[]{:S(2)}) %copy-start.2) | copy-done | bytes 131096
  4.4 0.0 copy-start.8
  4.4 0.7 %copy-done.8 = f32[32]{0:T(128)S(1)} copy-done((f32[32]{0:T(128)S(1)}, f32[32]{0:T(128)}, u32[]{:S(2)}) %copy-start.8) | copy-done | bytes 152
  5.0 55.6 %shard_map.104 = (f32[1,128,8,128]{3,2,1,0:T(8,128)S(1)}, f32[2,4]{1,0:T(2,128)S(1)}) custom-call(bf16[4,4,4096]{2,1,0:T(4,128)(2,1)S(1)} %copy-done.2, s32[2,4]{1,0:T(2,128)S(1)} %bitcast.3, s32[2,4]{1,0:T(2,128)S(1)} %bitcast.4, s32[4]{0:T(128)S(1)} %copy-done.5, s32[4]{0:T(128)S(1)} %copy-done.6, f32[64]{0:T(128)S(1)} %copy-done.7, f32[32]{0:T(128)S(1)} %copy-done.8, ...), custom_call_target="tpu_custom_call" | custom-call | tf_op jit(solution)/shard_map/pallas_call | solution.py:474
  60.6 0.8 %copy.13 = f32[1,128,8,128]{3,2,1,0:T(8,128)} copy(f32[1,128,8,128]{3,2,1,0:T(8,128)S(1)} %get-tuple-element.8) | data formatting | bytes 1048576
  61.4 0.6 copy.14
Async XLA Ops:
  0.6 0.7 %copy-start.4 = (s32[4,2]{0,1:T(2,128)S(1)}, s32[4,2]{0,1:T(2,128)}, u32[]{:S(2)}) copy-start(s32[4,2]{0,1:T(2,128)} %param.11) | copy-start | bytes 100
  0.6 0.7 %copy-start.6 = (s32[4]{0:T(128)S(1)}, s32[4]{0:T(128)}, u32[]{:S(2)}) copy-start(s32[4]{0:T(128)} %tid.1) | copy-start | bytes 52
  0.7 0.7 %copy-start.7 = (f32[64]{0:T(128)S(1)}, f32[64]{0:T(128)}, u32[]{:S(2)}) copy-start(f32[64]{0:T(128)} %focus.1) | copy-start | bytes 772
  0.7 0.7 %copy-start.3 = (s32[4,2]{0,1:T(2,128)S(1)}, s32[4,2]{0,1:T(2,128)}, u32[]{:S(2)}) copy-start(s32[4,2]{0,1:T(2,128)} %param.10) | copy-start | bytes 100
  0.7 0.7 %copy-start.5 = (s32[4]{0:T(128)S(1)}, s32[4]{0:T(128)}, u32[]{:S(2)}) copy-start(s32[4]{0:T(128)} %cidx.1) | copy-start | bytes 52
  1.4 1.0 %copy-start = (f32[1,8,128,128]{3,2,1,0:T(8,128)S(1)}, f32[1,8,128,128]{3,2,1,0:T(8,128)}, u32[]{:S(2)}) copy-start(f32[1,8,128,128]{3,2,1,0:T(8,128)} %maps.1) | copy-start | bytes 1572868
  2.4 1.0 %copy-start.1 = (bf16[16,128,128]{2,1,0:T(8,128)(2,1)S(1)}, bf16[16,128,128]{2,1,0:T(8,128)(2,1)}, u32[]{:S(2)}) copy-start(bf16[16,128,128]{2,1,0:T(8,128)(2,1)} %constant.2.clone.tab) | copy-start | bytes 1572868
  3.4 0.9 %copy-start.2 = (bf16[4,4,4096]{2,1,0:T(4,128)(2,1)S(1)}, bf16[4,4,4096]{2,1,0:T(4,128)(2,1)}, u32[]{:S(2)}) copy-start(bf16[4,4,4096]{2,1,0:T(4,128)(2,1)} %part.1) | copy-start | bytes 393220
  4.4 0.7 %copy-start.8 = (f32[32]{0:T(128)S(1)}, f32[32]{0:T(128)}, u32[]{:S(2)}) copy-start(f32[32]{0:T(128)} %gain.1) | copy-start | bytes 388

commit v2 on v1

v2 whole, which is shorter than its diff:
```python
import functools
import math

import jax
import jax.numpy as jnp
import numpy as np
from jax import lax
from jax.experimental import pallas as pl
from jax.experimental.pallas import tpu as pltpu
from jax.sharding import PartitionSpec as P

L = 128
BOX = 64
K = 2
P_DEV = 4
PLANES = 4
TAU_REG = 0.1
PHASE_SHIFT = 0.1
F32 = jnp.float32
BF16 = jnp.bfloat16
VMEM_BYTES = 63 * 2**20


def wrap(index, size):
    return jnp.where(index < size // 2, index, index - size)


def fast_sin(x):
    turns = jnp.floor(x * (1.0 / math.pi) + 0.5)
    r = x - turns * 3.140625
    r = r - turns * 9.67653589793e-4
    odd = turns - 2.0 * jnp.floor(turns * 0.5)
    r = r * (1.0 - 2.0 * odd)
    s = r * r
    poly = -1.0 / 39916800.0
    for c in (1.0 / 362880.0, -1.0 / 5040.0, 1.0 / 120.0, -1.0 / 6.0):
        poly = poly * s + c
    return r + r * s * poly


def split(x):
    high = x.astype(BF16)
    return high, (x - high.astype(F32)).astype(BF16)


def dot(a, b):
    return jnp.dot(a, b, preferred_element_type=F32)


def dot3(a, b):
    return dot(a[0], b[0]) + (dot(a[0], b[1]) + dot(a[1], b[0]))


def tables(n_slab):
    def cas(rows, cols):
        angle = (np.outer(rows, cols) % L) * (2.0 * math.pi / L)
        return (np.cos(angle) + np.sin(angle)) / math.sqrt(L)

    points = np.arange(L)
    wrapped = np.where(np.arange(BOX) < BOX // 2, np.arange(BOX), np.arange(BOX) - BOX)
    rows = cas(points, points)
    window = cas(wrapped, points)
    q = np.arange(2 * PLANES * n_slab)
    s, r = q // (2 * PLANES), q % (2 * PLANES)
    low = s * PLANES + r
    low = np.where(low < BOX // 2, low, low - BOX)
    freq = np.where(r < PLANES, low, BOX // 2 + s * PLANES + r - PLANES)
    planes = cas(points, freq)
    full = np.zeros((L, L))
    full[:, : len(q)] = planes
    picked = np.zeros((L, L))
    half = 2 * n_slab
    for jj in range(2):
        for row in range(half):
            picked[:, jj * half + row] = planes[:, (row // 2) * 2 * PLANES + 2 * (row % 2) + jj]
    none = np.zeros((BOX, L))
    negate = np.zeros((L, L))
    for block in range(2):
        for a in range(BOX):
            negate[block * BOX + a, block * BOX + (-a) % BOX] = 1.0
    first = np.concatenate([window.T, window.T], axis=1) / 64.0
    mats = [
        rows * TAU_REG,
        rows,
        full,
        picked,
        first,
        np.concatenate([window, none]),
        np.concatenate([none, window]),
        negate,
    ]
    pairs = []
    for mat in mats:
        mat = mat.astype(np.float32)
        high = mat.astype(jnp.bfloat16)
        pairs += [high, (mat - high.astype(np.float32)).astype(jnp.bfloat16)]
    return np.stack(pairs)


def kernel(
    sizes,
    part_hbm,
    cls_hbm,
    ori_hbm,
    cidx_hbm,
    tid_hbm,
    focus_hbm,
    gain_hbm,
    maps_hbm,
    tab_hbm,
    out,
    score_out,
    part,
    cls,
    ori,
    cidx,
    tid,
    focus,
    gain,
    maps,
    tab,
    tmp,
    xs,
    send_z,
    recv_z,
    send_y,
    recv_y,
    send_m,
    meta_z,
    meta_y,
    send1,
    recv1,
    acc,
    wrot,
    wtop,
    wz,
    wy,
    ctf,
    sums,
    scz_send,
    scz_recv,
    scy_send,
    scy_recv,
    ss_send,
    ss_recv,
    dlow,
    dhigh,
    rs_low,
    rs_high,
    red,
    dfull,
    send2,
    recv2,
    vbuf,
    in_sem,
    map_s,
    map_r,
    dom_s,
    dom_r,
    slab_s,
    slab_r,
):
    n_dom, n_map, n_slab = sizes
    n = n_map
    rows = L // n_slab
    chunk = BOX // n_dom
    d, m, s = lax.axis_index("dom"), lax.axis_index("map"), lax.axis_index("slab")

    def remote(to, src, dst, ssem, rsem):
        return pltpu.make_async_remote_copy(
            src_ref=src,
            dst_ref=dst,
            send_sem=ssem,
            recv_sem=rsem,
            device_id=to,
            device_id_type=pl.DeviceIdType.MESH,
        )

    loads = [
        pltpu.make_async_copy(here, there, in_sem.at[i])
        for i, (here, there) in enumerate(
            [
                (part_hbm, part),
                (cls_hbm, cls),
                (ori_hbm, ori),
                (cidx_hbm, cidx),
                (tid_hbm, tid),
                (focus_hbm, focus),
                (gain_hbm, gain),
                (maps_hbm, maps),
                (tab_hbm, tab),
            ]
        )
    ]
    for load in loads[:7]:
        load.start()

    barrier = pltpu.get_barrier_semaphore()

    def greet(to):
        pl.semaphore_signal(barrier, inc=1, device_id=to, device_id_type=pl.DeviceIdType.MESH)

    for step in range(1, n):
        greet({"map": lax.rem(m + step, n)})
        greet({"dom": lax.rem(d + step, n)})
    for step in range(n):

        @pl.when(jnp.logical_or(d != m, step != m))
        def _():
            greet({"dom": m, "map": jnp.int32(step)})

    for step in range(1, n_slab):
        greet({"slab": lax.rem(s + step, n_slab)})
    for load in loads[7:]:
        load.start()

    lane = lax.broadcasted_iota(jnp.int32, (L, L), 1)
    row = lax.broadcasted_iota(jnp.int32, (L, L), 0)
    lane8 = lax.broadcasted_iota(jnp.int32, (8, L), 1)
    row8 = lax.broadcasted_iota(jnp.int32, (8, L), 0)

    loads[0].wait()
    for g in range(2):
        both = jnp.concatenate([part[2 * g].astype(F32), part[2 * g + 1].astype(F32)], axis=0)
        up = pltpu.roll(both, 7, 0)
        for k in range(BOX // 2):
            here, above = both[:, k * L : (k + 1) * L], up[:, k * L : (k + 1) * L]
            even = jnp.where(lane8 < BOX, here, pltpu.roll(above, BOX, 1))
            odd = jnp.where(lane8 < BOX, pltpu.roll(here, BOX, 1), above)
            tmp[k] = jnp.where(row8 % 2 == 0, even, pltpu.roll(odd, 1, 0))
        for i in range(4):
            for h in range(2):
                start = (i % 2) * BOX + h
                xs[2 * g + i // 2, pl.ds(start, BOX // 2, stride=2), :] = tmp[:, 2 * i + h, :]
    for load in loads[1:7]:
        load.wait()

    META, DATA, SCORE, SUM, ALL, WIN = (i * n for i in range(6))

    def meta_copy(axis, c):
        to, there, ssem, rsem = ({"map": c}, meta_z.at[m], map_s, map_r) if axis == "map" else ({"dom": c}, meta_y.at[d], dom_s, dom_r)
        me = m if axis == "map" else d
        return remote(to, send_m.at[c], there, ssem.at[META + c], rsem.at[META + me])

    def data_copy(axis, c):
        if axis == "map":
            return remote({"map": c}, send_z.at[c], recv_z.at[m], map_s.at[DATA + c], map_r.at[DATA + m])
        return remote({"dom": c}, send_y.at[c], recv_y.at[d], dom_s.at[DATA + c], dom_r.at[DATA + d])

    def build(c, carry):
        found = jnp.int32(0)
        who = [jnp.int32(0)] * 2
        turn = [jnp.int32(0)] * 2
        for p in range(P_DEV):
            for j in range(K):
                hit = cls[j, p] == c
                for k in range(2):
                    mine = jnp.logical_and(hit, found == k)
                    who[k] = jnp.where(mine, p, who[k])
                    turn[k] = jnp.where(mine, ori[j, p], turn[k])
                found = found + hit.astype(jnp.int32)
        meta = jnp.zeros((8, L), F32)
        for k in range(2):
            power = jnp.where(found > k, gain[tid[who[k]]], 0.0)
            meta = jnp.where(row8 == 4 * k, focus[cidx[who[k]]], meta)
            meta = jnp.where(row8 == 4 * k + 1, power, meta)
            meta = jnp.where(row8 == 4 * k + 2, turn[k].astype(F32), meta)
            send_z[c, k * BOX : (k + 1) * BOX, :] = xs[who[k], :BOX].astype(BF16)
            send_y[c, k * BOX : (k + 1) * BOX, :] = xs[who[k], BOX:].astype(BF16)
        send_m[c] = meta
        return carry

    lax.fori_loop(0, n, build, 0)

    ahead_m = [lax.rem(m + step, n) for step in range(n)]
    ahead_d = [lax.rem(d + step, n) for step in range(n)]
    ahead_s = [lax.rem(s + step, n_slab) for step in range(n_slab)]
    order = [o for step in range(1, n // 2 + 1) for o in ([step] if 2 * step == n else [step, n - step])]

    def each_map(act):
        for step in order:
            act(ahead_m[step])

    def each_dom(act):
        for step in order:
            act(ahead_d[step])

    def each_slab(act):
        for t in ahead_s[1:]:
            act(t)

    others = (n_dom - 1) + (n_map - 1) + (n_slab - 1)
    pl.semaphore_wait(barrier, others + n - (d == m).astype(jnp.int32))

    for step in order[::-1]:
        data_copy("map", ahead_m[step]).start()
        data_copy("dom", ahead_d[step]).start()
    each_map(lambda c: meta_copy("map", c).start())
    each_dom(lambda c: meta_copy("dom", c).start())

    loads[7].wait()
    lane64 = lane[:BOX]
    halves = []
    for jp in range(2):
        cut = []
        for jj in range(2):
            plane = maps[0, 2 * jp + jj]
            cut.append(jnp.concatenate([plane[: BOX // 2], plane[L - BOX // 2 :]], axis=0))
        first = jnp.where(lane64 < BOX // 2, cut[0], pltpu.roll(cut[0], BOX, 1))
        second = jnp.where(lane64 < L - BOX // 2, pltpu.roll(cut[1], BOX, 1), cut[1])
        halves.append(jnp.where(lane64 < BOX, first, second))
    wtop[0] = halves[0]
    wtop[1] = halves[1]

    def piece_copy(c):
        return remote(
            {"map": c},
            wtop.at[1, pl.ds(pl.multiple_of(d * chunk, chunk), chunk)],
            wz.at[m],
            map_s.at[WIN + c],
            map_r.at[WIN + m],
        )

    each_map(lambda c: piece_copy(c).start())
    wz[m] = wtop[1, pl.ds(pl.multiple_of(d * chunk, chunk), chunk)]

    loads[8].wait()

    def table(i):
        return tab[2 * i], tab[2 * i + 1]

    for q in range(2 * PLANES):
        across = dot3(split(maps[0, q]), table(0))
        send1[:, q, :] = dot3(table(1), split(across))

    FIRST, SPREAD, SECOND = (i * n_slab for i in range(3))

    def first_copy(t):
        return remote(
            {"slab": t},
            send1.at[pl.ds(t * rows, rows)],
            recv1.at[:, pl.ds(pl.multiple_of(s * 2 * PLANES, 2 * PLANES), 2 * PLANES), :],
            slab_s.at[FIRST + t],
            slab_r.at[FIRST + s],
        )

    each_slab(lambda t: first_copy(t).start())
    recv1[:, pl.ds(pl.multiple_of(s * 2 * PLANES, 2 * PLANES), 2 * PLANES), :] = send1[pl.ds(s * rows, rows)]

    def window_copy(c):
        return remote(
            {"dom": c},
            wz.at[c],
            wy.at[pl.ds(pl.multiple_of(d * chunk, chunk), chunk)],
            dom_s.at[WIN + c],
            dom_r.at[WIN + d],
        )

    each_map(lambda c: remote({"map": c}, wz.at[c], wz.at[c], map_s.at[WIN + c], map_r.at[WIN + c]).wait_recv())
    each_dom(lambda c: window_copy(c).start())
    wy[pl.ds(pl.multiple_of(d * chunk, chunk), chunk)] = wz[d]

    fj = wrap(s * PLANES + 2 * (row // BOX) + lane // BOX, BOX)
    fa, fb = wrap(row % BOX, BOX), wrap(lane % BOX, BOX)
    squares = (fj * fj + fa * fa + fb * fb).astype(F32) * (1.0 / (BOX * BOX))

    def contrast(from_z, from_y, slot, total):
        for k in range(2):
            value = from_z[4 * k + 1 : 4 * k + 2] * fast_sin(from_z[4 * k : 4 * k + 1] * squares + PHASE_SHIFT)
            other = from_y[4 * k + 1 : 4 * k + 2] * fast_sin(from_y[4 * k : 4 * k + 1] * squares[BOX:] + PHASE_SHIFT)
            ctf[slot, k, :BOX] = value[:BOX]
            ctf[slot, k, BOX:] = other
            total = total + value * value
        return total

    power = contrast(send_m[m], send_m[d], 0, jnp.zeros((L, L), F32))

    def other_contrast(step, total):
        i, j = lax.rem(m + step, n), lax.rem(d + step, n)
        return contrast(meta_z[i], meta_y[j], step, total)

    each_map(lambda i: remote({"map": i}, send_m.at[i], meta_z.at[i], map_s.at[META + i], map_r.at[META + i]).wait_recv())
    each_dom(lambda j: remote({"dom": j}, send_m.at[j], meta_y.at[j], dom_s.at[META + j], dom_r.at[META + j]).wait_recv())
    power = lax.fori_loop(1, n, other_contrast, power)

    negate = tab[14]

    def by_left(x):
        high, lower = split(x)
        return dot(negate, high) + dot(negate, lower)

    def by_right(x):
        high, lower = split(x)
        return dot(high, negate) + dot(lower, negate)

    def swapped(x):
        t = x.T
        other = pltpu.roll(pltpu.roll(t, BOX, 0), BOX, 1)
        return jnp.where(row // BOX == lane // BOX, t, other)

    for jp in range(2):
        dlow[jp] = wtop[jp] * power[jp * BOX : (jp + 1) * BOX]

    sums[...] = jnp.zeros_like(sums)

    def collect(data, meta, slot, base):
        at = slice(base, base + BOX)
        for k in range(2):
            z = data[k * BOX : (k + 1) * BOX].astype(F32) * ctf[slot, k, at]
            turn = meta[4 * k + 2 : 4 * k + 3]
            for o in range(4):
                sums[o, at] += jnp.where(turn == float(o), z, 0.0)

    collect(send_z[m], send_m[m], 0, 0)
    collect(send_y[d], send_m[d], 0, BOX)

    for step in order:
        p, q = ahead_m[step], ahead_d[step]
        remote({"map": p}, send_z.at[p], recv_z.at[p], map_s.at[DATA + p], map_r.at[DATA + p]).wait_recv()
        collect(recv_z[p], meta_z[p], step, 0)
        remote({"dom": q}, send_y.at[q], recv_y.at[q], dom_s.at[DATA + q], dom_r.at[DATA + q]).wait_recv()
        collect(recv_y[q], meta_y[q], step, BOX)

    turned = swapped(by_left(sums[1]) + by_right(sums[3]))
    turned = turned + sums[0] + by_left(by_right(sums[2]))
    dlow[0] = dlow[0] - turned[:BOX]
    dhigh[...] = -turned[BOX:]

    def low_copy(c):
        return remote(
            {"dom": c},
            dlow.at[:, pl.ds(pl.multiple_of(c * chunk, chunk), chunk), :],
            rs_low.at[d],
            dom_s.at[SUM + c],
            dom_r.at[SUM + d],
        )

    def high_copy(c):
        return remote(
            {"dom": c, "map": d},
            dhigh.at[pl.ds(pl.multiple_of(c * chunk, chunk), chunk)],
            rs_high.at[m],
            map_s.at[SUM + c],
            map_r.at[SUM + m],
        )

    def unless_self(step, act):
        if step == 0:
            pl.when(d != m)(act)
        else:
            act()

    for step in range(n):
        c = lax.rem(d + step, n)
        if step:
            low_copy(c).start()
        unless_self(step, lambda c=c: high_copy(c).start())
    rs_low[d] = dlow[:, pl.ds(pl.multiple_of(d * chunk, chunk), chunk), :]

    @pl.when(d == m)
    def _():
        rs_high[m] = dhigh[pl.ds(pl.multiple_of(d * chunk, chunk), chunk)]

    def wait_window(c):
        piece = wy.at[pl.ds(pl.multiple_of(c * chunk, chunk), chunk)]
        remote({"dom": c}, piece, piece, dom_s.at[WIN + c], dom_r.at[WIN + c]).wait_recv()

    each_dom(wait_window)
    window = jnp.concatenate([wtop[0], wy[...]], axis=0)
    window_n = by_right(window)
    wrot[0] = window
    wrot[1] = swapped(window_n)
    wrot[2] = by_left(window_n)
    wrot[3] = swapped(by_left(window))

    def correlate(data, meta, slot, base):
        lines = jnp.zeros((8, L), F32)
        at = slice(base, base + BOX)
        for k in range(2):
            turn = meta[4 * k + 2 : 4 * k + 3]
            chosen = wrot[3, at]
            for o in (2, 1, 0):
                chosen = jnp.where(turn == float(o), wrot[o, at], chosen)
            found = data[k * BOX : (k + 1) * BOX].astype(F32) * ctf[slot, k, at] * chosen
            lines = jnp.where(row8 == k, jnp.sum(found, axis=0, keepdims=True), lines)
        return lines * (1.0 / BOX**1.5)

    scz_recv[m] = correlate(send_z[m], send_m[m], 0, 0)
    scy_recv[d] = correlate(send_y[d], send_m[d], 0, BOX)

    def score(step, carry):
        p, q = lax.rem(m + step, n), lax.rem(d + step, n)
        scz_send[p] = correlate(recv_z[p], meta_z[p], step, 0)
        scy_send[q] = correlate(recv_y[q], meta_y[q], step, BOX)
        return carry

    lax.fori_loop(1, n, score, 0)

    def score_copies(step):
        p, q = lax.rem(m + step, n), lax.rem(d + step, n)
        return [
            remote({"map": p}, scz_send.at[p], scz_recv.at[m], map_s.at[SCORE + p], map_r.at[SCORE + m]),
            remote({"dom": q}, scy_send.at[q], scy_recv.at[d], dom_s.at[SCORE + q], dom_r.at[SCORE + d]),
        ]

    for step in range(1, n):
        for copy in score_copies(step):
            copy.start()

    for step in range(1, n):
        c = lax.rem(d + step, n)
        remote({"dom": c}, rs_low.at[c], rs_low.at[c], dom_s.at[SUM + c], dom_r.at[SUM + c]).wait_recv()
    for c in range(n):

        @pl.when(jnp.logical_or(d != m, c != m))
        def _():
            piece = rs_high.at[c]
            remote({"dom": m, "map": jnp.int32(c)}, piece, piece, map_s.at[SUM + c], map_r.at[SUM + c]).wait_recv()

    total = rs_low[0]
    high = rs_high[0]
    for i in range(1, n):
        total = total + rs_low[i]
        high = high + rs_high[i]
    red[0] = total[0]
    red[1] = total[1] + high

    def all_copy(c):
        return remote(
            {"dom": c},
            red,
            dfull.at[:, pl.ds(pl.multiple_of(d * chunk, chunk), chunk), :],
            dom_s.at[ALL + c],
            dom_r.at[ALL + d],
        )

    for step in range(1, n):
        all_copy(lax.rem(d + step, n)).start()
    dfull[:, pl.ds(pl.multiple_of(d * chunk, chunk), chunk), :] = red[...]

    for step in range(1, n):
        p, q = lax.rem(m + step, n), lax.rem(d + step, n)
        remote({"map": p}, scz_send.at[p], scz_recv.at[p], map_s.at[SCORE + p], map_r.at[SCORE + p]).wait_recv()
        remote({"dom": q}, scy_send.at[q], scy_recv.at[q], dom_s.at[SCORE + q], dom_r.at[SCORE + q]).wait_recv()
    flat = [jnp.sum(scz_recv[:, k, :] + scy_recv[:, k, :], axis=1, keepdims=True) for k in range(2)]
    lane_m = lax.broadcasted_iota(jnp.int32, (n_map, L), 1)
    ss_send[...] = jnp.where(lane_m == 0, flat[0], jnp.where(lane_m == 1, flat[1], 0.0))

    def spread_copy(t):
        return remote({"slab": t}, ss_send, ss_recv.at[s], slab_s.at[SPREAD + t], slab_r.at[SPREAD + s])

    each_slab(lambda t: spread_copy(t).start())
    ss_recv[s] = ss_send[...]

    for step in range(1, n):
        c = lax.rem(d + step, n)
        piece = dfull.at[:, pl.ds(pl.multiple_of(c * chunk, chunk), chunk), :]
        remote({"dom": c}, red, piece, dom_s.at[ALL + c], dom_r.at[ALL + c]).wait_recv()

    for jp in range(2):
        columns = dot3(
            (tab[8][:, :BOX], tab[9][:, :BOX]), split(dfull[jp])
        )
        send2[:, jp] = columns.reshape(n_slab, rows, L)

    def second_copy(t):
        return remote({"slab": t}, send2.at[t], recv2.at[s], slab_s.at[SECOND + t], slab_r.at[SECOND + s])

    each_slab(lambda t: second_copy(t).start())
    recv2[s] = send2[s]

    def wait_first(t):
        there = recv1.at[:, pl.ds(pl.multiple_of(t * 2 * PLANES, 2 * PLANES), 2 * PLANES), :]
        remote({"slab": t}, send1.at[pl.ds(t * rows, rows)], there, slab_s.at[FIRST + t], slab_r.at[FIRST + t]).wait_recv()

    each_slab(wait_first)
    deep = 2 * PLANES * n_slab
    by_plane = (tab[4][:, :deep], tab[5][:, :deep])
    for y in range(rows):
        acc[y] = dot3(by_plane, split(recv1[y]))

    def sent_map(c):
        meta_copy("map", c).wait_send()
        data_copy("map", c).wait_send()
        piece_copy(c).wait_send()

    def sent_dom(c):
        meta_copy("dom", c).wait_send()
        data_copy("dom", c).wait_send()
        window_copy(c).wait_send()
        low_copy(c).wait_send()
        all_copy(c).wait_send()

    def sent_slab(t):
        first_copy(t).wait_send()
        spread_copy(t).wait_send()

    each_map(sent_map)
    each_dom(sent_dom)
    each_slab(sent_slab)
    for step in range(n):
        c = lax.rem(d + step, n)
        unless_self(step, lambda c=c: high_copy(c).wait_send())
        if step:
            for copy in score_copies(step):
                copy.wait_send()

    each_slab(
        lambda t: remote({"slab": t}, ss_send, ss_recv.at[t], slab_s.at[SPREAD + t], slab_r.at[SPREAD + t]).wait_recv()
    )
    tally = ss_recv[0]
    for i in range(1, n_slab):
        tally = tally + ss_recv[i]
    row_m = lax.broadcasted_iota(jnp.int32, (n_map, L), 0)
    out_row = lax.broadcasted_iota(jnp.int32, (K, P_DEV), 0)
    out_col = lax.broadcasted_iota(jnp.int32, (K, P_DEV), 1)
    found = jnp.zeros((K, P_DEV), F32)
    for p in range(P_DEV):
        for i in range(K):
            c = cls[i, p]
            rank = jnp.int32(0)
            for e in range(p * K + i):
                rank = rank + (cls[e % K, e // K] == c).astype(jnp.int32)
            here = jnp.logical_and(row_m == c, lane_m == rank)
            one = jnp.sum(jnp.where(here, tally, 0.0), axis=0, keepdims=True)
            one = jnp.sum(one, axis=1, keepdims=True)
            found = jnp.where(jnp.logical_and(out_row == i, out_col == p), one, found)
    score_out[...] = found

    each_slab(
        lambda t: remote({"slab": t}, send2.at[t], recv2.at[t], slab_s.at[SECOND + t], slab_r.at[SECOND + t]).wait_recv()
    )
    lines = split(recv2[...].reshape(n_slab * 2 * rows, L))
    half = 2 * n_slab
    for jj in range(2):
        vbuf[jj * half : (jj + 1) * half] = dot3(lines, table(5 + jj)).reshape(half, rows, L)
    by_low = (tab[6][:, : 2 * half], tab[7][:, : 2 * half])
    for y in range(rows):
        out[0, :, y, :] = acc[y] + dot3(by_low, split(vbuf[:, y, :]))

    each_slab(lambda t: second_copy(t).wait_send())


def solution(mesh):
    n_dom, n_map, n_slab = (mesh.shape[a] for a in ("dom", "map", "slab"))
    rows, chunk = L // n_slab, BOX // n_dom
    tab = tables(n_slab)
    vmem = pl.BlockSpec(memory_space=pltpu.VMEM)
    hbm = pl.BlockSpec(memory_space=pltpu.HBM)
    dma = pltpu.SemaphoreType.DMA

    def local(particles, class_list, orient, ctf_index, tomo_id, defocus, tomo_gain, maps):
        args = (particles, class_list.T, orient.T, ctf_index, tomo_id, defocus, tomo_gain, maps, tab)
        spaces = [pltpu.VMEM] + [pltpu.SMEM] * 6 + [pltpu.VMEM] * 2
        real_grad, scores = pl.pallas_call(
            functools.partial(kernel, (n_dom, n_map, n_slab)),
            out_shape=(
                jax.ShapeDtypeStruct((1, L, rows, L), F32),
                jax.ShapeDtypeStruct((K, P_DEV), F32),
            ),
            in_specs=[hbm] * len(args),
            out_specs=(vmem, vmem),
            scratch_shapes=[space(arg.shape, arg.dtype) for space, arg in zip(spaces, args)]
            + [
                pltpu.VMEM((BOX // 2, 8, L), F32),
                pltpu.VMEM((P_DEV, L, L), F32),
            ]
            + [pltpu.VMEM((n_map, L, L), BF16)] * 4
            + [pltpu.VMEM((n_map, 8, L), F32)] * 3
            + [
                pltpu.VMEM((L, 2 * PLANES, L), F32),
                pltpu.VMEM((rows, 2 * PLANES * n_slab, L), F32),
                pltpu.VMEM((rows, L, L), F32),
                pltpu.VMEM((4, L, L), F32),
                pltpu.VMEM((2, BOX, L), F32),
                pltpu.VMEM((n_map, chunk, L), F32),
                pltpu.VMEM((BOX, L), F32),
                pltpu.VMEM((n_map, 2, L, L), F32),
                pltpu.VMEM((4, L, L), F32),
            ]
            + [pltpu.VMEM((n_map, 8, L), F32)] * 4
            + [
                pltpu.VMEM((n_map, L), F32),
                pltpu.VMEM((n_slab, n_map, L), F32),
                pltpu.VMEM((2, BOX, L), F32),
                pltpu.VMEM((BOX, L), F32),
                pltpu.VMEM((n_dom, 2, chunk, L), F32),
                pltpu.VMEM((n_map, chunk, L), F32),
                pltpu.VMEM((2, chunk, L), F32),
                pltpu.VMEM((2, BOX, L), F32),
                pltpu.VMEM((n_slab, 2, rows, L), F32),
                pltpu.VMEM((n_slab, 2, rows, L), F32),
                pltpu.VMEM((4 * n_slab, rows, L), F32),
                dma((len(args),)),
            ]
            + [dma((6 * n_map,))] * 4
            + [dma((3 * n_slab,))] * 2,
            compiler_params=pltpu.CompilerParams(
                collective_id=0, has_side_effects=True, vmem_limit_bytes=VMEM_BYTES
            ),
        )(*args)
        return real_grad, scores.T

    pair = P(("dom", "map"))
    return jax.shard_map(
        local,
        mesh=mesh,
        in_specs=(
            P(("dom", "map"), "slab", None),
            pair,
            pair,
            pair,
            pair,
            P(),
            P(),
            P("map", "slab", None, None),
        ),
        out_specs=(P("map", None, "slab", None), pair),
        check_vma=False,
    )
```

time: 62.3 us -> 61.6 us (0.989)
  local copies, waits for them, and re-layouts: 5.69 us -> 2.44 us
  Pallas kernels: 55.6 us -> 58.4 us
    unnamed x20 -> x4, local copies, waits for them, and re-layouts: 5.69 us -> 2.44 us
    pallas_call x1, Pallas kernels: 55.6 us -> 58.4 us  [local(): pl.pallas_call(functools.partial(kernel, (n_dom, n_map, n_slab)), out_sha...]
where the time goes in v2:
time: 61.6 us; the launch traced here: 61.5 us
  Pallas kernels  58.4 us (95%)
  local copies, waits for them, and re-layouts  2.44 us (4%)
  between operations  0.65 us (1%)
    pallas_call x1, Pallas kernels, local(): pl.pallas_call(functools.partial(kernel, (n_dom, n_map, n_slab)), out_sha...  58.4 us
    unnamed x4, local copies, waits for them, and re-layouts  2.44 us

profile of v2, /device:TPU:1, one launch (start us, length us, event | category | flops | bytes accessed | tf_op | source)
XLA Modules:
  0.0 61.5 jit_solution(11633511271018141148)
XLA Ops:
  0.6 58.4 %shard_map.104 = (f32[1,128,8,128]{3,2,1,0:T(8,128)}, f32[2,4]{1,0:T(2,128)}) custom-call(bf16[4,4,4096]{2,1,0:T(4,128)(2,1)} %part_hbm.1, s32[2,4]{1,0:T(2,128)} %bitcast.3, s32[2,4]{1,0:T(2,128)} %bitcast.4, s32[4]{0:T(128)} %cidx_hbm.1, s32[4]{0:T(128)} %tid_hbm.1, f32[64]{0:T(128)} %focus_hbm.1, f32[32]{0:T(128)} %gain_hbm.1, ...), custom_call_target="tpu_custom_call" | custom-call | tf_op jit(solution)/shard_map/pallas_call | solution.py:655
  59.0 0.0 copy-start
  59.0 1.9 %copy.13 = f32[1,128,8,128]{3,2,1,0:T(8,128)} copy(f32[1,128,8,128]{3,2,1,0:T(8,128)} %get-tuple-element.8) | data formatting | bytes 1048576
  60.9 0.0 copy-done
  60.9 0.6 copy.14
Async XLA Ops:
  59.0 1.9 %copy-start = (f32[2,4]{1,0:T(2,128)S(1)}, f32[2,4]{1,0:T(2,128)}, u32[]{:S(2)}) copy-start(f32[2,4]{1,0:T(2,128)} %get-tuple-element.5) | copy-start | bytes 100
